TPU v7x, 32 devices: a whole 2x2x4 slice. The times are simulated.
32 devices in a mesh: wide: 16 (over z, y, core), narrow: 2 (over x).
Axes of the slice: x: 2, y: 2, z: 4, core: 2. Of those that a mesh axis runs over, the one named last changes fastest.
Arguments:
- tokens: bfloat16 [128, 128, 768], P(('wide', 'narrow')), may hold values from -6 to 6
- land_mask: int32 [128, 128], P(('wide', 'narrow')), may hold values from 0 to 1, as said below
- cotangent: bfloat16 [128, 128, 768], P(('wide', 'narrow')), may hold values from -6 to 6
- qkv_weight: bfloat16 [768, 2304], replicated, may hold values from -0.21875 to 0.21875
- query_bias: float32 [768], replicated, may hold values from -3 to 3
- value_bias: float32 [768], replicated, may hold values from -3 to 3
- proj_weight: bfloat16 [768, 768], replicated, may hold values from -0.625 to 0.625
- proj_bias: float32 [768], replicated, may hold values from -3 to 3
- up_weight: bfloat16 [768, 3072], replicated, may hold values from -0.21875 to 0.21875
- up_bias: float32 [3072], replicated, may hold values from -3 to 3
- down_weight: bfloat16 [3072, 768], replicated, may hold values from -0.109375 to 0.109375
- down_bias: float32 [768], replicated, may hold values from -3 to 3
- norm1_gain: float32 [768], replicated, may hold values from 0.1 to 1.9
- norm1_shift: float32 [768], replicated, may hold values from -2 to 2
- norm2_gain: float32 [768], replicated, may hold values from 0.1 to 1.9
- norm2_shift: float32 [768], replicated, may hold values from -2 to 2
Outputs:
- output: bfloat16 [128, 128, 768], P(('wide', 'narrow'))
- tokens_grad: float32 [128, 128, 768], P(('wide', 'narrow'))
- qkv_grad: float32 [768, 2304], P('wide', 'narrow')
- query_bias_grad: float32 [768], replicated
- value_bias_grad: float32 [768], replicated
- proj_grad: float32 [768, 768], P('wide', 'narrow')
- proj_bias_grad: float32 [768], replicated
- up_grad: float32 [768, 3072], P('wide', 'narrow')
- up_bias_grad: float32 [3072], replicated
- down_grad: float32 [3072, 768], P('wide', 'narrow')
- down_bias_grad: float32 [768], replicated
- norm1_gain_grad: float32 [768], replicated
- norm1_shift_grad: float32 [768], replicated
- norm2_gain_grad: float32 [768], replicated
- norm2_shift_grad: float32 [768], replicated
Inputs may be any that keep to these rules, and one draw needn't show every extreme that they name: `land_mask`: every field holds at least one land patch; in every draw one field is all land and another holds a single land patch; which slots are land is random.
All inputs are finite; a program needn't handle non-finite values.
Results may differ from a plain program's by a relative error of at most 0.012.
Values sent between devices are 32-bit elements; how exact they have to be, the bound alone decides.
A program may use at most 192 MiB of HBM per device.

v0:
```python
import jax
import jax.numpy as jnp
from jax import lax
from jax.experimental import pallas as pl
from jax.experimental.pallas import tpu as pltpu
from jax.sharding import PartitionSpec as P

HEADS = 12
F32 = jnp.float32
BF16 = jnp.bfloat16
SLOTS = 6
LAGS = (0, 2, 4, 6)
LEAD = 3
UNROLL = 3


def dot(a, b):
    return lax.dot_general(a, b, (((1,), (0,)), ((), ())), preferred_element_type=F32)


def dot_nt(a, b):
    return lax.dot_general(a, b, (((1,), (1,)), ((), ())), preferred_element_type=F32)


def dot_tn(a, b):
    return lax.dot_general(a, b, (((0,), (0,)), ((), ())), preferred_element_type=F32)


def standardise(rows):
    centred = rows - jnp.mean(rows, -1, keepdims=True)
    scale = lax.rsqrt(jnp.mean(centred * centred, -1, keepdims=True) + 1e-06)
    return centred * scale, scale


def norm_back(unit_rows, scale, pulled):
    return scale * (
        pulled
        - jnp.mean(pulled, -1, keepdims=True)
        - unit_rows * jnp.mean(pulled * unit_rows, -1, keepdims=True)
    )


def column_sums(rows):
    return jnp.sum(rows, axis=0, keepdims=True)


def layer_kernel(wide, narrow, fields, patches, *refs):
    (
        tokens_in, cotangent_in, qkv_in, proj_in, up_in, down_in, land_in,
    ) = refs[:7]
    vectors_in, refs = refs[7:16], refs[16:]
    (
        output_out, tokens_out, qkv_out, proj_out, up_out, down_out, vec_out,
        tok, cot, n1, qkv, att, mid, n2, act_t, acts, hgrs, acc, ngr, left, w_a, w_b, w_p, qkv_bias, flat,
        keep, core_in, up_sums, up_sum, down_sum, proj_sum, qkv_sum, in_0, in_1, in_2, in_3, vec, vec_in,
        load_sem, core_send, core_recv, core_free, stage_send, stage_recv, final_sem,
        vec_send, vec_recv, store_sem, land,
    ) = refs[:-9]
    vectors_held = refs[-9:]
    (
        query_bias, value_bias, proj_bias, up_bias, down_bias,
        gain_one, shift_one, gain_two, shift_two,
    ) = vectors_held
    model = tok.shape[1]
    hidden_width = w_a.shape[1]
    stage_in = (in_0, in_1, in_2, in_3)
    act, hgr = acts.at[0], hgrs.at[0]
    at_wide = lax.axis_index("wide")
    at_narrow = lax.axis_index("narrow")
    width = model // narrow
    block_rows = model // wide
    group_rows = block_rows // 3
    chunk = width
    parts = 36

    def my_bit(axis, level):
        index = at_wide if axis == "wide" else at_narrow
        return lax.rem(lax.div(index, 1 << level), 2)

    def partner(axis, level):
        shift = (1 << level) * (1 - 2 * my_bit(axis, level))
        if axis == "wide":
            return (at_wide + shift, at_narrow)
        return (at_wide, at_narrow + shift)

    wide_bits = [("wide", i) for i in range(1, wide.bit_length() - 1)]
    narrow_bits = [("narrow", i) for i in range(narrow.bit_length() - 1)]
    all_bits = [("wide", 0)] + wide_bits + narrow_bits
    stages = len(wide_bits) + len(narrow_bits)
    blocks = 1 << stages
    core = my_bit("wide", 0)
    mine = {bit: my_bit(*bit) for bit in all_bits}
    to = {bit: partner(*bit) for bit in all_bits}

    def order(part, group):
        if group == 0:
            return narrow_bits + wide_bits
        if group == 1:
            return wide_bits[:1] + narrow_bits + wide_bits[1:]
        if part % 2 == 0:
            return wide_bits[1:2] + narrow_bits + wide_bits[:1] + wide_bits[2:]
        return wide_bits[1:2] + wide_bits[:1] + narrow_bits + wide_bits[2:]

    def place(part, group, row_block, column_block):
        found = 0
        for axis, level in order(part, group):
            index = row_block if axis == "wide" else column_block
            found = 2 * found + ((index >> level) & 1)
        return found

    barrier = pltpu.get_barrier_semaphore()
    for bit in all_bits:
        pl.semaphore_signal(
            barrier, inc=1, device_id=to[bit], device_id_type=pl.DeviceIdType.MESH
        )

    def remote(src, dst, send, recv, bit):
        return pltpu.make_async_remote_copy(
            src_ref=src, dst_ref=dst, send_sem=send, recv_sem=recv,
            device_id=to[bit], device_id_type=pl.DeviceIdType.MESH,
        )

    def kept_slot(part):
        return part % (3 * SLOTS)

    def sent_slot(part):
        return 3 * SLOTS + part % 6

    def core_copy(part):
        slot = part % 6
        return remote(
            keep.at[sent_slot(part)], core_in.at[slot],
            core_send.at[slot], core_recv.at[slot], ("wide", 0),
        )

    def core_start(part):
        if part >= 6:
            pl.semaphore_wait(core_free, 1)
        core_copy(part).start()

    def span(part, group, stage):
        half = blocks >> (stage + 1)
        sequence = order(part, group)
        base = 0
        for earlier in range(stage):
            base = base + mine[sequence[earlier]] * (blocks >> (earlier + 1))
        bit = sequence[stage]
        return half, base + mine[bit] * half, base + (1 - mine[bit]) * half, bit

    gaps = [LEAD] + [LAGS[i] - LAGS[i - 1] for i in range(1, 4)]
    cycle = [2 * (gap + gap % 2) for gap in gaps]

    def stage_copy(part, group, stage):
        half, own, other, bit = span(part, group, stage)
        sent = sum(gaps[:stage]) + part % gaps[stage]
        held = sum(cycle[:stage]) + part % cycle[stage]
        return remote(
            keep.at[kept_slot(part), group, pl.ds(other, half)],
            stage_in[stage].at[part % cycle[stage], group],
            stage_send.at[sent, group],
            stage_recv.at[held, group],
            bit,
        )

    def core_end(part):
        slot = part % 6
        core_copy(part).wait()
        keep[kept_slot(part)] += core_in[slot]
        if part + 6 < parts:
            pl.semaphore_signal(
                core_free, inc=1, device_id=to[("wide", 0)],
                device_id_type=pl.DeviceIdType.MESH,
            )
        for group in range(3):
            stage_copy(part, group, 0).start()

    def result_place(part, group):
        unit, row = part // 3, (part % 3) * group_rows
        if unit < 4:
            return up_sum, row, unit * width + group * 128
        if unit < 8:
            return down_sum, (unit - 4) * block_rows + row, group * 128
        if unit == 8:
            return proj_sum, row, group * 128
        return qkv_sum, row, (unit - 9) * width + group * 128

    def stage_end(part, stage):
        for group in range(3):
            stage_copy(part, group, stage).wait()
            half, own, other, bit = span(part, group, stage)
            slot, came = kept_slot(part), stage_in[stage].at[part % cycle[stage], group]
            if stage + 1 < stages:
                keep[slot, group, pl.ds(own, half)] += came[...]
                stage_copy(part, group, stage + 1).start()
            else:
                ref, row, column = result_place(part, group)
                ref[row : row + group_rows, column : column + 128] = (
                    keep[slot, group, own] + came[0]
                )

    result_copies = [
        pltpu.make_async_copy(src, dst, final_sem.at[number])
        for number, (src, dst) in enumerate(
            ((up_sum, up_out), (down_sum, down_out), (proj_sum, proj_out), (qkv_sum, qkv_out))
        )
    ]
    last_part = {11: 0, 23: 1, 26: 2, 35: 3}

    def tick(number):
        for stage in reversed(range(stages)):
            part = number - LAGS[stage]
            if 0 <= part < parts:
                stage_end(part, stage)
                if stage + 1 == stages and part in last_part:
                    result_copies[last_part[part]].start()

    def make_unit(unit, lhs_half, rhs):
        half_blocks = wide // 2

        def one(half, carry):
            product = dot(lhs_half(half), rhs())
            for third in range(3):
                part = 3 * unit + third
                kept, sent = kept_slot(part), sent_slot(part)
                index = [kept + core * (sent - kept), sent + core * (kept - sent)]
                for row_block in range(half_blocks):
                    top = row_block * block_rows + third * group_rows
                    for column_block in range(narrow):
                        for group in range(3):
                            first = place(part, group, row_block, column_block)
                            step = place(part, group, half_blocks, 0)
                            side = column_block * width + group * 128
                            keep[index[row_block % 2], group, first + half * step] = product[
                                top : top + group_rows, side : side + 128
                            ]
            return carry

        lax.fori_loop(0, 2, one, 0)
        for third in range(3):
            core_start(3 * unit + third)

    def row_of(vector):
        return vector[...].reshape(1, vector.shape[0])

    def load(src, dst, number):
        copy = pltpu.make_async_copy(src, dst, load_sem.at[number])
        copy.start()
        return copy

    tok_load = load(tokens_in, tok, 0)
    qkv_load = load(qkv_in, w_a.at[:, pl.ds(0, 3 * model)], 1)
    small_loads = [load(land_in, land, 6)] + [
        load(src, dst, 7 + number)
        for number, (src, dst) in enumerate(zip(vectors_in, vectors_held))
    ]
    vec[...] = jnp.zeros_like(vec)
    acc[...] = jnp.zeros_like(acc)
    ngr[...] = jnp.zeros_like(ngr)
    for small in small_loads:
        small.wait()
    qkv_bias[:, 0:model] = row_of(query_bias)
    qkv_bias[:, model : 2 * model] = jnp.zeros((1, model), F32)
    qkv_bias[:, 2 * model :] = row_of(value_bias)
    for number, vector in enumerate(
        (proj_bias, down_bias, gain_one, shift_one, gain_two, shift_two)
    ):
        flat[number : number + 1, 0:model] = row_of(vector)
    flat[6:7, :] = row_of(up_bias)

    def field_rows(field):
        return pl.ds(pl.multiple_of(field * patches, patches), patches)

    def each_field(step):
        def body(field, carry):
            step(field)
            return carry

        lax.fori_loop(0, fields, body, 0)

    tok_load.wait()
    at_model = pl.ds(0, model)
    proj_row, down_row, gain_one_row, shift_one_row, gain_two_row, shift_two_row = (
        flat.at[pl.ds(number, 1), at_model] for number in range(6)
    )
    up_row = flat.at[pl.ds(6, 1), :]

    def norm_one(field):
        rows = field_rows(field)
        unit_rows, scale = standardise(tok[rows, :].astype(F32))
        n1[rows, :] = (unit_rows * gain_one_row[...] + shift_one_row[...]).astype(BF16)

    each_field(norm_one)
    qkv_load.wait()
    proj_load = load(proj_in, w_p, 2)
    cot_load = load(cotangent_in, cot, 3)
    down_load = load(down_in, w_b, 4)

    def project(tile, carry):
        columns = pl.ds(pl.multiple_of(tile * 256, 256), 256)
        qkv[:, columns] = (dot(n1[...], w_a[:, columns]) + qkv_bias[:, columns]).astype(BF16)
        return carry

    lax.fori_loop(0, 3 * model // 256, project, 0)
    up_load = load(up_in, w_a, 5)

    lane = lax.broadcasted_iota(jnp.int32, (1, 128), 1)
    head_masks = [(lane < 64).astype(BF16), (lane >= 64).astype(BF16)]
    lane_full = lax.broadcasted_iota(jnp.int32, (patches, 128), 1)
    pairs = model // 128

    def stack_heads(rows, factor=1.0):
        return jnp.concatenate([rows * (mask * BF16(factor)) for mask in head_masks], 0)

    def pick_heads(rows):
        return jnp.where(lane_full < 64, rows[:patches], rows[patches:])

    def soften(stacked, key_rows, visible):
        scores = jnp.where(visible, dot_nt(stacked, key_rows), -1e30)
        exponent = jnp.exp(scores - jnp.max(scores, -1, keepdims=True))
        return exponent * (1.0 / jnp.sum(exponent, -1, keepdims=True))

    def pair_columns(pair):
        return [pl.ds(part * model + pair * 128, 128) for part in range(3)]

    def visible_of(field):
        return jnp.broadcast_to(land[pl.ds(field, 1), :], (2 * patches, patches)) > 0

    def attend(field):
        rows = field_rows(field)
        visible = visible_of(field)
        for pair in range(pairs):
            at_q, at_k, at_v = pair_columns(pair)
            attention = soften(stack_heads(qkv[rows, at_q], 0.125), qkv[rows, at_k], visible)
            both = dot(attention.astype(BF16), qkv[rows, at_v])
            att[rows, pl.ds(pair * 128, 128)] = pick_heads(both).astype(BF16)

    each_field(attend)
    proj_load.wait()

    def residual(tile, carry):
        columns = pl.ds(pl.multiple_of(tile * 256, 256), 256)
        mid[:, columns] = (
            tok[:, columns].astype(F32) + dot(att[...], w_p[:, columns]) + proj_row[:, columns]
        )
        return carry

    lax.fori_loop(0, model // 256, residual, 0)

    def norm_two(field):
        rows = field_rows(field)
        unit_rows, scale = standardise(mid[rows, :])
        normed = (unit_rows * gain_two_row[...] + shift_two_row[...]).astype(BF16)
        n2[rows, :] = normed
        left[:, rows] = normed.T

    each_field(norm_two)

    root = 0.7978845608028654

    def hidden_columns(part, column_block):
        return pl.multiple_of(column_block * (hidden_width // narrow) + part * chunk, chunk)

    def each_block(step):
        def body(column_block, carry):
            step(column_block)
            return carry

        lax.fori_loop(0, narrow, body, 0)

    def feed(part):
        def one(column_block):
            first = hidden_columns(part, column_block)
            columns = pl.ds(first, chunk)
            here = pl.ds(pl.multiple_of(column_block * chunk, chunk), chunk)
            hidden = dot(n2[...], w_a[:, columns]) + up_row[:, columns]
            pulled = dot_nt(cot[...], w_b[columns, :])
            square = hidden * hidden
            bent = jnp.tanh(hidden * (root + (root * 0.044715) * square))
            cdf = 0.5 + 0.5 * bent
            activated = (hidden * cdf).astype(BF16)
            slope = cdf + (hidden * (0.5 - 0.5 * bent * bent)) * (
                root + (3 * root * 0.044715) * square
            )
            grad = (pulled * slope).astype(BF16)
            acts[part, :, here] = activated
            hgrs[part, :, here] = grad
            act_t[columns, :] = activated.T
            up_sums[:, columns] = column_sums(grad.astype(F32))

        each_block(one)

    def feed_sums(part):
        def one(column_block):
            columns = pl.ds(hidden_columns(part, column_block), chunk)
            here = pl.ds(pl.multiple_of(column_block * chunk, chunk), chunk)
            acc[...] += dot(acts[part, :, here], w_b[columns, :])
            ngr[...] += dot_nt(hgrs[part, :, here], w_a[:, columns])

        each_block(one)

    def left_half(half):
        return left[pl.ds(pl.multiple_of(half * (model // 2), model // 2), model // 2), :]

    def up_unit(part):
        make_unit(part, left_half, lambda: hgrs[part])

    def down_unit(part):
        def rows(half):
            first = half * (hidden_width // 2) + part * block_rows
            return jnp.concatenate(
                [
                    act_t[
                        pl.ds(pl.multiple_of(first + block * 4 * block_rows, 16), block_rows), :
                    ]
                    for block in range(wide // 2)
                ],
                0,
            )

        make_unit(4 + part, rows, lambda: cot[...])

    def store_output(field):
        rows = field_rows(field)
        act[rows, :] = (mid[rows, :] + acc[rows, :] + down_row[...]).astype(BF16)

    output_copy = pltpu.make_async_copy(act, output_out, store_sem.at[0])
    tokens_copy = pltpu.make_async_copy(acc, tokens_out, store_sem.at[1])

    def add_sums(row, columns, rows):
        vec[pl.ds(row, 1), columns] += column_sums(rows)

    everything = pl.ds(0, model)

    def middle_back(field):
        rows = field_rows(field)
        unit_rows, scale = standardise(mid[rows, :])
        grads = ngr[rows, :]
        top = cot[rows, :].astype(F32)
        add_sums(7, everything, top)
        add_sums(10, everything, grads * unit_rows)
        add_sums(11, everything, grads)
        total = top + norm_back(unit_rows, scale, grads * gain_two_row[...])
        acc[rows, :] = total
        low = total.astype(BF16)
        hgr[rows, :] = low
        add_sums(2, everything, low.astype(F32))

    def attend_back(field, first_pair, last_pair):
        rows = field_rows(field)
        visible = visible_of(field)

        def one(pair, carry):
            here = pl.multiple_of(pair * 128, 128)
            at_q, at_k, at_v = (pl.ds(step * model + here, 128) for step in range(3))
            key_rows, values = qkv[rows, at_k], qkv[rows, at_v]
            stacked = stack_heads(qkv[rows, at_q], 0.125)
            attention = soften(stacked, key_rows, visible)
            pulled = stack_heads(act[rows, pl.ds(here, 128)])
            values_grad = dot_tn(attention.astype(BF16), pulled).astype(BF16)
            inner = dot_nt(pulled, values)
            inner = inner - jnp.sum(attention * inner, -1, keepdims=True)
            scores_grad = (attention * inner).astype(BF16)
            queries_grad = (pick_heads(dot(scores_grad, key_rows)) * 0.125).astype(BF16)
            keys_grad = dot_tn(scores_grad, stacked).astype(BF16)
            qkv[rows, at_q] = queries_grad
            qkv[rows, at_k] = keys_grad
            qkv[rows, at_v] = values_grad
            add_sums(0, pl.ds(here, 128), queries_grad.astype(F32))
            add_sums(1, pl.ds(here, 128), values_grad.astype(F32))
            return carry

        lax.fori_loop(first_pair, last_pair, one, 0, unroll=UNROLL)

    def turn(source):
        for field in range(fields):
            left[:, field_rows(field)] = source[field_rows(field), :].T

    def proj_unit():
        turn(att)
        make_unit(8, left_half, lambda: hgr[...])

    def qkv_unit(part):
        stride = 3 * model // narrow
        make_unit(
            9 + part,
            left_half,
            lambda: jnp.concatenate(
                [
                    qkv[:, pl.ds(block * stride + part * width, width)]
                    for block in range(narrow)
                ],
                1,
            ),
        )

    def source_back(field):
        rows = field_rows(field)
        unit_rows, scale = standardise(tok[rows, :].astype(F32))
        grads = ngr[rows, :]
        add_sums(8, everything, grads * unit_rows)
        add_sums(9, everything, grads)
        acc[rows, :] += norm_back(unit_rows, scale, grads * gain_one_row[...])

    def vec_copy(number):
        return remote(
            vec, vec_in.at[number], vec_send.at[number], vec_recv.at[number], all_bits[number]
        )

    def vec_end(number):
        vec_copy(number).wait()
        vec[...] += vec_in[number]
        if number + 1 < len(all_bits):
            vec_copy(number + 1).start()

    def make_attended_grad():
        output_copy.wait()
        act[...] = dot_nt(hgr[...], w_p[...]).astype(BF16)

    def finish_output():
        for number in range(hidden_width // model):
            vec[3 + number : 4 + number, :] = up_sums[:, number * model : (number + 1) * model]
        each_field(store_output)
        output_copy.start()

    qkv_again = pltpu.make_async_copy(qkv_in, w_a.at[:, pl.ds(0, 3 * model)], load_sem.at[1])

    def make_normed_grad(half):
        columns = pl.ds(half * (model // 2), model // 2)
        if half == 0:
            qkv_again.wait()
        ngr[:, columns] = dot_nt(qkv[...], w_a[columns, pl.ds(0, 3 * model)])

    def finish_tokens():
        each_field(source_back)
        tokens_copy.start()
        vec_copy(0).start()

    def some(step, *values):
        return lambda: step(*values)

    halves = [(0, pairs // 2), (pairs // 2, pairs)]
    backs = [
        some(attend_back, field, *half) for field in range(fields) for half in halves
    ]
    backs_at = {13: 1, 15: 1, 16: 1, 18: 1, 19: 1, 21: 1, 22: 2}
    work = {
        0: [some(feed, 2)],
        1: [some(feed_sums, 0)],
        2: [some(up_unit, 2)],
        3: [some(feed, 3)],
        5: [some(up_unit, 3)],
        6: [some(feed_sums, 1)],
        7: [some(feed_sums, 2)],
        8: [some(down_unit, 0)],
        9: [some(feed_sums, 3), qkv_again.start],
        10: [finish_output],
        11: [some(down_unit, 1)],
        12: [some(each_field, middle_back), make_attended_grad],
        14: [some(down_unit, 2)],
        17: [some(down_unit, 3)],
        20: [proj_unit],
        23: [some(turn, n1), some(qkv_unit, 0)],
        24: [some(make_normed_grad, 0)],
        25: [some(make_normed_grad, 1)],
        26: [some(qkv_unit, 1)],
        27: [finish_tokens],
        29: [some(qkv_unit, 2)],
    }
    for number, count in backs_at.items():
        work[number] = [backs.pop(0) for _ in range(count)]
    for number in range(len(all_bits)):
        work.setdefault(30 + 2 * number, []).append(some(vec_end, number))

    up_load.wait()
    down_load.wait()
    cot_load.wait()
    feed(0)
    pl.semaphore_wait(barrier, len(all_bits))
    up_unit(0)
    core_end(0)
    core_end(1)
    core_end(2)
    feed(1)
    up_unit(1)
    vec_store = pltpu.make_async_copy(vec, vec_out, store_sem.at[2])
    for number in range(parts + LAGS[-1]):
        for step in work.get(number, []):
            step()
        tick(number)
        if 0 <= number + LEAD < parts:
            core_end(number + LEAD)
        if number == 30 + 2 * (len(all_bits) - 1):
            vec_store.start()
    for copy in result_copies:
        copy.wait()
    tokens_copy.wait()
    vec_store.wait()


def place_results(*refs):
    arrays, vec, placed, vectors, (sem, *held) = refs[:6], refs[6], refs[7:13], refs[13:22], refs[22:]
    inward = [
        pltpu.make_async_copy(src, dst, sem.at[0, number])
        for number, (src, dst) in enumerate(zip(arrays, held))
    ]
    outward = [
        pltpu.make_async_copy(src, dst, sem.at[1, number])
        for number, (src, dst) in enumerate(zip(held, placed))
    ]
    for copy in inward:
        copy.start()
    row = 0
    for vector in vectors:
        model = vec.shape[1]
        for part in range(vector.shape[0] // model):
            vector[pl.ds(part * model, model)] = vec[row, :]
            row += 1
    for before, after in zip(inward, outward):
        before.wait()
        after.start()
    for copy in outward:
        copy.wait()


def local_fused(wide, narrow, *args):
    (
        tokens, land_mask, cotangent, qkv_weight, query_bias, value_bias, proj_weight, proj_bias,
        up_weight, up_bias, down_weight, down_bias, norm1_gain, norm1_shift, norm2_gain, norm2_shift,
    ) = args
    fields, patches, model = tokens.shape
    rows = fields * patches
    hidden_width = up_weight.shape[1]
    width, block_rows = model // narrow, model // wide
    bits = (wide * narrow).bit_length() - 1
    blocks = wide * narrow // 2
    group_rows = block_rows // 3
    gaps = [LEAD] + [LAGS[i] - LAGS[i - 1] for i in range(1, 4)]
    cycle = [2 * (gap + gap % 2) for gap in gaps]
    anywhere = pl.BlockSpec(memory_space=pl.ANY)
    in_vmem = pl.BlockSpec(memory_space=pltpu.VMEM)

    def vmem(shape, dtype=F32):
        return pltpu.VMEM(shape, dtype)

    dma = pltpu.SemaphoreType.DMA
    vectors = [model] * 3 + [hidden_width] + [model] * 5
    results = pl.pallas_call(
        lambda *refs: layer_kernel(wide, narrow, fields, patches, *refs),
        out_shape=[
            jax.ShapeDtypeStruct((rows, model), BF16),
            jax.ShapeDtypeStruct((rows, model), F32),
            jax.ShapeDtypeStruct((block_rows, 3 * width), F32),
            jax.ShapeDtypeStruct((block_rows, width), F32),
            jax.ShapeDtypeStruct((block_rows, 4 * width), F32),
            jax.ShapeDtypeStruct((4 * block_rows, width), F32),
            jax.ShapeDtypeStruct((16, model), F32),
        ],
        in_specs=[anywhere] * 16,
        out_specs=[anywhere] * 7,
        scratch_shapes=[
            vmem((rows, model), BF16),
            vmem((rows, model), BF16),
            vmem((rows, model), BF16),
            vmem((rows, 3 * model), BF16),
            vmem((rows, model), BF16),
            vmem((rows, model)),
            vmem((rows, model), BF16),
            vmem((hidden_width, rows), BF16),
            vmem((4, rows, model), BF16),
            vmem((4, rows, model), BF16),
            vmem((rows, model)),
            vmem((rows, model)),
            vmem((model, rows), BF16),
            vmem((model, hidden_width), BF16),
            vmem((hidden_width, model), BF16),
            vmem((model, model), BF16),
            vmem((1, 3 * model)),
            vmem((8, hidden_width)),
            vmem((3 * SLOTS + 6, 3, blocks, group_rows, 128)),
            vmem((6, 3, blocks, group_rows, 128)),
            vmem((1, hidden_width)),
            vmem((block_rows, 4 * width)),
            vmem((4 * block_rows, width)),
            vmem((block_rows, width)),
            vmem((block_rows, 3 * width)),
            *[vmem((cycle[s], 3, blocks >> (s + 1), group_rows, 128)) for s in range(4)],
            vmem((16, model)),
            vmem((bits, 16, model)),
            dma((16,)),
            dma((6,)),
            dma((6,)),
            pltpu.SemaphoreType.REGULAR,
            dma((sum(gaps), 3)),
            dma((sum(cycle), 3)),
            dma((4,)),
            dma((bits,)),
            dma((bits,)),
            dma((3,)),
            vmem((fields, patches), jnp.int32),
            *[vmem((size,)) for size in vectors],
        ],
        compiler_params=pltpu.CompilerParams(
            collective_id=0, has_side_effects=True, vmem_limit_bytes=63 << 20
        ),
        name="encoder_layer",
    )(
        tokens.reshape(rows, model),
        cotangent.reshape(rows, model),
        qkv_weight,
        proj_weight,
        up_weight,
        down_weight,
        land_mask,
        query_bias,
        value_bias,
        proj_bias,
        up_bias,
        down_bias,
        norm1_gain,
        norm1_shift,
        norm2_gain,
        norm2_shift,
    )
    placed = pl.pallas_call(
        place_results,
        out_shape=[jax.ShapeDtypeStruct(array.shape, array.dtype) for array in results[:6]]
        + [jax.ShapeDtypeStruct((size,), F32) for size in vectors],
        in_specs=[anywhere] * 6 + [in_vmem],
        out_specs=[anywhere] * 6 + [in_vmem] * 9,
        scratch_shapes=[dma((2, 6))] + [vmem(array.shape, array.dtype) for array in results[:6]],
        name="place_results",
    )(*results)
    output, tokens_grad, qkv_grad, proj_grad, up_grad, down_grad = placed[:6]
    (
        query_grad, value_grad, proj_bias_grad, up_bias_grad, down_bias_grad,
        gain_one_grad, shift_one_grad, gain_two_grad, shift_two_grad,
    ) = placed[6:]
    return (
        output.reshape(tokens.shape),
        tokens_grad.reshape(tokens.shape),
        qkv_grad,
        query_grad,
        value_grad,
        proj_grad,
        proj_bias_grad,
        up_grad,
        up_bias_grad,
        down_grad,
        down_bias_grad,
        gain_one_grad,
        shift_one_grad,
        gain_two_grad,
        shift_two_grad,
    )


def layer_norm(inputs, norm_gain, norm_shift):
    average = jnp.mean(inputs, -1, keepdims=True)
    centred = inputs - average
    variance = jnp.mean(centred * centred, -1, keepdims=True)
    return centred * lax.rsqrt(variance + 1e-06) * norm_gain + norm_shift


def attend_scores(queries, key_rows, visible, scaling):
    scores = (
        jnp.einsum("fqhe,fkhe->fhqk", queries, key_rows, preferred_element_type=jnp.float32)
        * scaling
    )
    return jnp.where(visible[:, None, None, :], scores, -1e30)


def share_sums(former, latter):
    row_sums = (
        lax.psum_scatter(former, "wide", scatter_dimension=0, tiled=True),
        lax.psum_scatter(latter, "wide", scatter_dimension=0, tiled=True),
    )
    return (
        lax.psum_scatter(row_sums[0], "narrow", scatter_dimension=1, tiled=True),
        lax.psum_scatter(row_sums[1], "narrow", scatter_dimension=1, tiled=True),
    )


def local(
    tokens,
    land_mask,
    cotangent,
    qkv_weight,
    query_bias,
    value_bias,
    proj_weight,
    proj_bias,
    up_weight,
    up_bias,
    down_weight,
    down_bias,
    norm1_gain,
    norm1_shift,
    norm2_gain,
    norm2_shift,
):
    field_count, length, model_width = tokens.shape
    head_count = HEADS
    head_width = model_width // head_count
    scaling = head_width ** (-0.5)
    visible = land_mask > 0
    split_shape = (field_count, length, head_count, head_width)
    source = tokens.astype(jnp.float32)
    normed_one = layer_norm(source, norm1_gain, norm1_shift).astype(jnp.bfloat16)
    joint = jnp.einsum("fpd,de->fpe", normed_one, qkv_weight, preferred_element_type=jnp.float32)
    queries = (joint[..., :model_width] + query_bias).astype(jnp.bfloat16).reshape(split_shape)
    key_rows = joint[..., model_width : 2 * model_width].astype(jnp.bfloat16).reshape(split_shape)
    values = (joint[..., 2 * model_width :] + value_bias).astype(jnp.bfloat16).reshape(split_shape)
    scores = attend_scores(queries, key_rows, visible, scaling)
    highest = jnp.max(scores, -1, keepdims=True)
    exponent = jnp.exp(scores - highest)
    summed = jnp.sum(exponent, -1, keepdims=True)
    attention = exponent / summed
    log_total = highest + jnp.log(summed)
    attended = jnp.einsum(
        "fhqk,fkhe->fqhe",
        attention.astype(jnp.bfloat16),
        values,
        preferred_element_type=jnp.float32,
    )
    attended = attended.reshape(field_count, length, model_width).astype(jnp.bfloat16)
    middle = (
        source
        + jnp.einsum("fpd,de->fpe", attended, proj_weight, preferred_element_type=jnp.float32)
        + proj_bias
    )
    normed_two = layer_norm(middle, norm2_gain, norm2_shift).astype(jnp.bfloat16)
    hidden = (
        jnp.einsum("fpd,dn->fpn", normed_two, up_weight, preferred_element_type=jnp.float32)
        + up_bias
    )
    activated_full, gelu_pull = jax.vjp(jax.nn.gelu, hidden)
    activated = activated_full.astype(jnp.bfloat16)
    output = (
        middle
        + jnp.einsum("fpn,nd->fpd", activated, down_weight, preferred_element_type=jnp.float32)
        + down_bias
    )
    grad_out = cotangent.astype(jnp.float32)
    down_local = jnp.einsum("fpn,fpd->nd", activated, cotangent, preferred_element_type=jnp.float32)
    down_bias_local = jnp.sum(grad_out, axis=(0, 1))
    activated_grad = jnp.einsum(
        "fpd,nd->fpn", cotangent, down_weight, preferred_element_type=jnp.float32
    )
    hidden_grad = gelu_pull(activated_grad)[0].astype(jnp.bfloat16)
    up_local = jnp.einsum(
        "fpd,fpn->dn", normed_two, hidden_grad, preferred_element_type=jnp.float32
    )
    up_bias_local = jnp.sum(hidden_grad.astype(jnp.float32), axis=(0, 1))
    feed_sums = share_sums(up_local, down_local)
    normed_two_grad = jnp.einsum(
        "fpn,dn->fpd", hidden_grad, up_weight, preferred_element_type=jnp.float32
    )
    unused_two, norm_two_pull = jax.vjp(layer_norm, middle, norm2_gain, norm2_shift)
    middle_part, gain_two_local, shift_two_local = norm_two_pull(normed_two_grad)
    middle_grad = grad_out + middle_part
    middle_low = middle_grad.astype(jnp.bfloat16)
    proj_local = jnp.einsum("fpd,fpe->de", attended, middle_low, preferred_element_type=jnp.float32)
    proj_bias_local = jnp.sum(middle_low.astype(jnp.float32), axis=(0, 1))
    attended_grad = jnp.einsum(
        "fpe,de->fpd", middle_low, proj_weight, preferred_element_type=jnp.float32
    )
    attended_grad = attended_grad.astype(jnp.bfloat16).reshape(split_shape)
    scores = attend_scores(queries, key_rows, visible, scaling)
    attention = jnp.exp(scores - log_total)
    values_grad = jnp.einsum(
        "fhqk,fqhe->fkhe",
        attention.astype(jnp.bfloat16),
        attended_grad,
        preferred_element_type=jnp.float32,
    )
    attention_grad = jnp.einsum(
        "fqhe,fkhe->fhqk", attended_grad, values, preferred_element_type=jnp.float32
    )
    inner_sum = jnp.sum(attention * attention_grad, -1, keepdims=True)
    scores_grad = (attention * (attention_grad - inner_sum)).astype(jnp.bfloat16)
    queries_grad = (
        jnp.einsum("fhqk,fkhe->fqhe", scores_grad, key_rows, preferred_element_type=jnp.float32)
        * scaling
    )
    keys_grad = (
        jnp.einsum("fhqk,fqhe->fkhe", scores_grad, queries, preferred_element_type=jnp.float32)
        * scaling
    )
    flat_shape = (field_count, length, model_width)
    joint_grad = jnp.concatenate(
        [
            queries_grad.reshape(flat_shape),
            keys_grad.reshape(flat_shape),
            values_grad.reshape(flat_shape),
        ],
        -1,
    ).astype(jnp.bfloat16)
    qkv_local = jnp.einsum(
        "fpd,fpe->de", normed_one, joint_grad, preferred_element_type=jnp.float32
    )
    joint_sums = jnp.sum(joint_grad.astype(jnp.float32), axis=(0, 1))
    query_bias_local = joint_sums[:model_width]
    value_bias_local = joint_sums[2 * model_width :]
    attention_sums = share_sums(qkv_local, proj_local)
    normed_one_grad = jnp.einsum(
        "fpe,de->fpd", joint_grad, qkv_weight, preferred_element_type=jnp.float32
    )
    unused_one, norm_one_pull = jax.vjp(layer_norm, source, norm1_gain, norm1_shift)
    source_part, gain_one_local, shift_one_local = norm_one_pull(normed_one_grad)
    tokens_grad = middle_grad + source_part
    vectors = lax.psum(
        (
            query_bias_local,
            value_bias_local,
            proj_bias_local,
            up_bias_local,
            down_bias_local,
            gain_one_local,
            shift_one_local,
            gain_two_local,
            shift_two_local,
        ),
        ("wide", "narrow"),
    )
    return (
        output.astype(jnp.bfloat16),
        tokens_grad,
        attention_sums[0],
        vectors[0],
        vectors[1],
        attention_sums[1],
        vectors[2],
        feed_sums[0],
        vectors[3],
        feed_sums[1],
        vectors[4],
        vectors[5],
        vectors[6],
        vectors[7],
        vectors[8],
    )


def solution(mesh):
    wide, narrow = mesh.shape["wide"], mesh.shape["narrow"]
    placed = (
        P(("wide", "narrow"), None, None),
        P(("wide", "narrow"), None),
        P(("wide", "narrow"), None, None),
        P(),
        P(),
        P(),
        P(),
        P(),
        P(),
        P(),
        P(),
        P(),
        P(),
        P(),
        P(),
        P(),
    )
    fused = (wide, narrow) == (16, 2)

    def layer(*args):
        return local_fused(wide, narrow, *args) if fused else local(*args)

    return jax.shard_map(
        layer,
        mesh=mesh,
        in_specs=placed,
        out_specs=(
            P(("wide", "narrow"), None, None),
            P(("wide", "narrow"), None, None),
            P("wide", "narrow"),
            P(),
            P(),
            P("wide", "narrow"),
            P(),
            P("wide", "narrow"),
            P(),
            P("wide", "narrow"),
            P(),
            P(),
            P(),
            P(),
            P(),
        ),
        check_vma=False,
    )
```

profile of v0, /device:TPU:0, one launch (start us, length us, event | category | flops | bytes accessed | tf_op | source)
XLA Modules:
  0.0 136.5 jit_solution(2383855494566749747)
XLA Ops:
  0.7 131.1 %encoder_layer.1 = (bf16[512,768]{1,0:T(8,128)(2,1)}, f32[512,768]{1,0:T(8,128)}, f32[48,1152]{1,0:T(8,128)}, f32[48,384]{1,0:T(8,128)}, f32[48,1536]{1,0:T(8,12...) custom-call(bf16[512,768]{1,0:T(8,128)(2,1)} %bitcast.4, bf16[512,768]{1,0:T(8,128)(2,1)} %bitcast.5, ...), custom_call_target="tpu_custom_call" | custom-call | tf_op jit(solution)/shard_map/encoder_layer/pallas_call | solution.py:647
  131.7 4.6 %place_results.1 = (bf16[512,768]{1,0:T(8,128)(2,1)}, f32[512,768]{1,0:T(8,128)}, f32[48,1152]{1,0:T(8,128)}, f32[48,384]{1,0:T(8,128)}, f32[48,1536]{1,0:T(8,12...) custom-call(bf16[512,768]{1,0:T(8,128)(2,1)} %get-tuple-element.37.r, ...), custom_call_target="tpu_custom_call" | custom-call | tf_op jit(solution)/shard_map/place_results/pallas_call | solution.py:724
where the time goes:
time: 137 us
  Pallas kernels  136 us (99%)
    pallas_call x1, Pallas kernels, local_fused(): pl.pallas_call(lambda *refs: layer_kernel(wide, narrow, fields, patches,...  131 us
    pallas_call x1, Pallas kernels, local_fused(): pl.pallas_call(place_results, out_shape=[jax.ShapeDtypeStruct(array.shape...  4.6 us

commit v1 on v0

--- a/solution.py
+++ b/solution.py
@@ -11,7 +11,8 @@
 SLOTS = 6
 LAGS = (0, 2, 4, 6)
 LEAD = 3
-UNROLL = 3
+TILE = 768
+FIRST = 9
 
 
 def dot(a, b):
@@ -206,8 +207,11 @@
     ]
     last_part = {11: 0, 23: 1, 26: 2, 35: 3}
 
-    def tick(number):
+    def tick(number, between=()):
         for stage in reversed(range(stages)):
+            if stage == 1:
+                for step in between:
+                    step()
             part = number - LAGS[stage]
             if 0 <= part < parts:
                 stage_end(part, stage)
@@ -296,11 +300,11 @@
     down_load = load(down_in, w_b, 4)
 
     def project(tile, carry):
-        columns = pl.ds(pl.multiple_of(tile * 256, 256), 256)
+        columns = pl.ds(pl.multiple_of(tile * TILE, TILE), TILE)
         qkv[:, columns] = (dot(n1[...], w_a[:, columns]) + qkv_bias[:, columns]).astype(BF16)
         return carry
 
-    lax.fori_loop(0, 3 * model // 256, project, 0)
+    lax.fori_loop(0, 3 * model // TILE, project, 0)
     up_load = load(up_in, w_a, 5)
 
     lane = lax.broadcasted_iota(jnp.int32, (1, 128), 1)
@@ -315,9 +319,12 @@
         return jnp.where(lane_full < 64, rows[:patches], rows[patches:])
 
     def soften(stacked, key_rows, visible):
-        scores = jnp.where(visible, dot_nt(stacked, key_rows), -1e30)
-        exponent = jnp.exp(scores - jnp.max(scores, -1, keepdims=True))
-        return exponent * (1.0 / jnp.sum(exponent, -1, keepdims=True))
+        scores = [dot_nt(one, keys) for one, keys in zip(stacked, key_rows)]
+        scores = [jnp.where(visible, one, -1e30) for one in scores]
+        tops = [jnp.max(one, -1, keepdims=True) for one in scores]
+        exponents = [jnp.exp(one - top) for one, top in zip(scores, tops)]
+        shares = [1.0 / jnp.sum(one, -1, keepdims=True) for one in exponents]
+        return [one * share for one, share in zip(exponents, shares)]
 
     def pair_columns(pair):
         return [pl.ds(part * model + pair * 128, 128) for part in range(3)]
@@ -328,11 +335,15 @@
     def attend(field):
         rows = field_rows(field)
         visible = visible_of(field)
+        at = [pair_columns(pair) for pair in range(pairs)]
+        stacked = [stack_heads(qkv[rows, at_q], 0.125) for at_q, at_k, at_v in at]
+        attention = soften(stacked, [qkv[rows, at_k] for at_q, at_k, at_v in at], visible)
+        both = [
+            dot(one.astype(BF16), qkv[rows, at_v])
+            for one, (at_q, at_k, at_v) in zip(attention, at)
+        ]
         for pair in range(pairs):
-            at_q, at_k, at_v = pair_columns(pair)
-            attention = soften(stack_heads(qkv[rows, at_q], 0.125), qkv[rows, at_k], visible)
-            both = dot(attention.astype(BF16), qkv[rows, at_v])
-            att[rows, pl.ds(pair * 128, 128)] = pick_heads(both).astype(BF16)
+            att[rows, pl.ds(pair * 128, 128)] = pick_heads(both[pair]).astype(BF16)
 
     each_field(attend)
     proj_load.wait()
@@ -449,27 +460,31 @@
         rows = field_rows(field)
         visible = visible_of(field)
 
-        def one(pair, carry):
-            here = pl.multiple_of(pair * 128, 128)
-            at_q, at_k, at_v = (pl.ds(step * model + here, 128) for step in range(3))
-            key_rows, values = qkv[rows, at_k], qkv[rows, at_v]
-            stacked = stack_heads(qkv[rows, at_q], 0.125)
-            attention = soften(stacked, key_rows, visible)
-            pulled = stack_heads(act[rows, pl.ds(here, 128)])
-            values_grad = dot_tn(attention.astype(BF16), pulled).astype(BF16)
-            inner = dot_nt(pulled, values)
-            inner = inner - jnp.sum(attention * inner, -1, keepdims=True)
-            scores_grad = (attention * inner).astype(BF16)
-            queries_grad = (pick_heads(dot(scores_grad, key_rows)) * 0.125).astype(BF16)
-            keys_grad = dot_tn(scores_grad, stacked).astype(BF16)
-            qkv[rows, at_q] = queries_grad
-            qkv[rows, at_k] = keys_grad
-            qkv[rows, at_v] = values_grad
-            add_sums(0, pl.ds(here, 128), queries_grad.astype(F32))
-            add_sums(1, pl.ds(here, 128), values_grad.astype(F32))
-            return carry
-
-        lax.fori_loop(first_pair, last_pair, one, 0, unroll=UNROLL)
+        some = range(first_pair, last_pair)
+        at = [pair_columns(pair) for pair in some]
+        here = [pl.ds(pair * 128, 128) for pair in some]
+        stacked = [stack_heads(qkv[rows, at_q], 0.125) for at_q, at_k, at_v in at]
+        pulled = [stack_heads(act[rows, columns]) for columns in here]
+        attention = soften(stacked, [qkv[rows, at_k] for at_q, at_k, at_v in at], visible)
+        inner = [dot_nt(one, qkv[rows, at_v]) for one, (at_q, at_k, at_v) in zip(pulled, at)]
+        inner = [
+            one - jnp.sum(share * one, -1, keepdims=True) for share, one in zip(attention, inner)
+        ]
+        scores_grad = [(share * one).astype(BF16) for share, one in zip(attention, inner)]
+        queries_grad = [
+            (pick_heads(dot(one, qkv[rows, at_k])) * 0.125).astype(BF16)
+            for one, (at_q, at_k, at_v) in zip(scores_grad, at)
+        ]
+        keys_grad = [dot_tn(one, rest).astype(BF16) for one, rest in zip(scores_grad, stacked)]
+        values_grad = [
+            dot_tn(one.astype(BF16), rest).astype(BF16) for one, rest in zip(attention, pulled)
+        ]
+        for number, (at_q, at_k, at_v) in enumerate(at):
+            qkv[rows, at_q] = queries_grad[number]
+            qkv[rows, at_k] = keys_grad[number]
+            qkv[rows, at_v] = values_grad[number]
+            add_sums(0, here[number], queries_grad[number].astype(F32))
+            add_sums(1, here[number], values_grad[number].astype(F32))
 
     def turn(source):
         for field in range(fields):
@@ -584,9 +599,10 @@
     up_unit(1)
     vec_store = pltpu.make_async_copy(vec, vec_out, store_sem.at[2])
     for number in range(parts + LAGS[-1]):
-        for step in work.get(number, []):
+        steps = work.get(number, [])
+        for step in steps[:FIRST]:
             step()
-        tick(number)
+        tick(number, steps[FIRST:])
         if 0 <= number + LEAD < parts:
             core_end(number + LEAD)
         if number == 30 + 2 * (len(all_bits) - 1):
@@ -598,27 +614,41 @@
 
 
 def place_results(*refs):
-    arrays, vec, placed, vectors, (sem, *held) = refs[:6], refs[6], refs[7:13], refs[13:22], refs[22:]
-    inward = [
-        pltpu.make_async_copy(src, dst, sem.at[0, number])
-        for number, (src, dst) in enumerate(zip(arrays, held))
+    arrays, vec_in, placed, vectors_out = refs[:6], refs[6], refs[7:13], refs[13:22]
+    in_sem, out_sem, vec_sem, vec, *held = refs[22:]
+    vectors, held = held[:9], held[9:]
+
+    def pieces(ref):
+        count = 4 if ref.shape[0] % 64 == 0 and ref.shape[0] >= 512 else 1
+        size = ref.shape[0] // count
+        return [pl.ds(number * size, size) for number in range(count)]
+
+    moves = [
+        (src.at[rows], mid.at[rows], dst.at[rows])
+        for src, mid, dst in zip(arrays, held, placed)
+        for rows in pieces(src)
     ]
-    outward = [
-        pltpu.make_async_copy(src, dst, sem.at[1, number])
-        for number, (src, dst) in enumerate(zip(held, placed))
-    ]
-    for copy in inward:
-        copy.start()
+    vec_copy = pltpu.make_async_copy(vec_in, vec, vec_sem.at[9])
+    vec_copy.start()
+    inward, outward = [], []
+    for number, (src, mid, dst) in enumerate(moves):
+        inward.append(pltpu.make_async_copy(src, mid, in_sem.at[number]))
+        outward.append(pltpu.make_async_copy(mid, dst, out_sem.at[number]))
+        inward[-1].start()
+    vec_copy.wait()
     row = 0
-    for vector in vectors:
+    vec_outward = []
+    for number, (vector, vector_out) in enumerate(zip(vectors, vectors_out)):
         model = vec.shape[1]
         for part in range(vector.shape[0] // model):
             vector[pl.ds(part * model, model)] = vec[row, :]
             row += 1
+        vec_outward.append(pltpu.make_async_copy(vector, vector_out, vec_sem.at[number]))
+        vec_outward[-1].start()
     for before, after in zip(inward, outward):
         before.wait()
         after.start()
-    for copy in outward:
+    for copy in outward + vec_outward:
         copy.wait()
 
 
@@ -637,7 +667,6 @@
     gaps = [LEAD] + [LAGS[i] - LAGS[i - 1] for i in range(1, 4)]
     cycle = [2 * (gap + gap % 2) for gap in gaps]
     anywhere = pl.BlockSpec(memory_space=pl.ANY)
-    in_vmem = pl.BlockSpec(memory_space=pltpu.VMEM)
 
     def vmem(shape, dtype=F32):
         return pltpu.VMEM(shape, dtype)
@@ -725,9 +754,11 @@
         place_results,
         out_shape=[jax.ShapeDtypeStruct(array.shape, array.dtype) for array in results[:6]]
         + [jax.ShapeDtypeStruct((size,), F32) for size in vectors],
-        in_specs=[anywhere] * 6 + [in_vmem],
-        out_specs=[anywhere] * 6 + [in_vmem] * 9,
-        scratch_shapes=[dma((2, 6))] + [vmem(array.shape, array.dtype) for array in results[:6]],
+        in_specs=[anywhere] * 7,
+        out_specs=[anywhere] * 15,
+        scratch_shapes=[dma((12,)), dma((12,)), dma((10,)), vmem((16, model))]
+        + [vmem((size,)) for size in vectors]
+        + [vmem(array.shape, array.dtype) for array in results[:6]],
         name="place_results",
     )(*results)
     output, tokens_grad, qkv_grad, proj_grad, up_grad, down_grad = placed[:6]

time: 137 us -> 134 us (0.978)
  Pallas kernels: 136 us -> 133 us
    pallas_call x1, Pallas kernels: 131 us -> 129 us  [local_fused(): pl.pallas_call(lambda *refs: layer_kernel(wide, narrow, fields, patches,...]
where the time goes in v1:
time: 134 us
  Pallas kernels  133 us (99%)
    pallas_call x1, Pallas kernels, local_fused(): pl.pallas_call(lambda *refs: layer_kernel(wide, narrow, fields, patches,...  129 us
    pallas_call x1, Pallas kernels, local_fused(): pl.pallas_call(place_results, out_shape=[jax.ShapeDtypeStruct(array.shape...  3.83 us

profile of v1, /device:TPU:0, one launch (start us, length us, event | category | flops | bytes accessed | tf_op | source)
XLA Modules:
  0.0 133.7 jit_solution(4191695898854130928)
XLA Ops:
  0.7 129.0 %encoder_layer.1 = (bf16[512,768]{1,0:T(8,128)(2,1)}, f32[512,768]{1,0:T(8,128)}, f32[48,1152]{1,0:T(8,128)}, f32[48,384]{1,0:T(8,128)}, f32[48,1536]{1,0:T(8,12...) custom-call(bf16[512,768]{1,0:T(8,128)(2,1)} %bitcast.4, bf16[512,768]{1,0:T(8,128)(2,1)} %bitcast.5, ...), custom_call_target="tpu_custom_call" | custom-call | tf_op jit(solution)/shard_map/encoder_layer/pallas_call | solution.py:676
  129.7 3.8 %place_results.1 = (bf16[512,768]{1,0:T(8,128)(2,1)}, f32[512,768]{1,0:T(8,128)}, f32[48,1152]{1,0:T(8,128)}, f32[48,384]{1,0:T(8,128)}, f32[48,1536]{1,0:T(8,12...) custom-call(bf16[512,768]{1,0:T(8,128)(2,1)} %get-tuple-element.37.r, ...), custom_call_target="tpu_custom_call" | custom-call | tf_op jit(solution)/shard_map/place_results/pallas_call | solution.py:753

commit v2 on v1

--- a/solution.py
+++ b/solution.py
@@ -11,7 +11,6 @@
 SLOTS = 6
 LAGS = (0, 2, 4, 6)
 LEAD = 3
-TILE = 768
 FIRST = 9
 
 
@@ -166,14 +165,14 @@
     def core_end(part):
         slot = part % 6
         core_copy(part).wait()
-        keep[kept_slot(part)] += core_in[slot]
+        for group in range(3):
+            keep[kept_slot(part), group] += core_in[slot, group]
+            stage_copy(part, group, 0).start()
         if part + 6 < parts:
             pl.semaphore_signal(
                 core_free, inc=1, device_id=to[("wide", 0)],
                 device_id_type=pl.DeviceIdType.MESH,
             )
-        for group in range(3):
-            stage_copy(part, group, 0).start()
 
     def result_place(part, group):
         unit, row = part // 3, (part % 3) * group_rows
@@ -252,10 +251,14 @@
         return copy
 
     tok_load = load(tokens_in, tok, 0)
-    qkv_load = load(qkv_in, w_a.at[:, pl.ds(0, 3 * model)], 1)
     small_loads = [load(land_in, land, 6)] + [
         load(src, dst, 7 + number)
         for number, (src, dst) in enumerate(zip(vectors_in, vectors_held))
+    ]
+    thirds = [pl.ds(number * model, model) for number in range(3)]
+    qkv_loads = [
+        load(qkv_in.at[:, columns], w_a.at[:, columns], number)
+        for columns, number in zip(thirds, (1, 16, 17))
     ]
     vec[...] = jnp.zeros_like(vec)
     acc[...] = jnp.zeros_like(acc)
@@ -294,17 +297,13 @@
         n1[rows, :] = (unit_rows * gain_one_row[...] + shift_one_row[...]).astype(BF16)
 
     each_field(norm_one)
-    qkv_load.wait()
-    proj_load = load(proj_in, w_p, 2)
-    cot_load = load(cotangent_in, cot, 3)
-    down_load = load(down_in, w_b, 4)
-
-    def project(tile, carry):
-        columns = pl.ds(pl.multiple_of(tile * TILE, TILE), TILE)
+    later_loads = []
+    for number, columns in enumerate(thirds):
+        qkv_loads[number].wait()
+        if number == 2:
+            later_loads += [load(proj_in, w_p, 2), load(cotangent_in, cot, 3), load(down_in, w_b, 4)]
         qkv[:, columns] = (dot(n1[...], w_a[:, columns]) + qkv_bias[:, columns]).astype(BF16)
-        return carry
-
-    lax.fori_loop(0, 3 * model // TILE, project, 0)
+    proj_load, cot_load, down_load = later_loads
     up_load = load(up_in, w_a, 5)
 
     lane = lax.broadcasted_iota(jnp.int32, (1, 128), 1)
@@ -592,10 +591,10 @@
     feed(0)
     pl.semaphore_wait(barrier, len(all_bits))
     up_unit(0)
+    feed(1)
     core_end(0)
     core_end(1)
     core_end(2)
-    feed(1)
     up_unit(1)
     vec_store = pltpu.make_async_copy(vec, vec_out, store_sem.at[2])
     for number in range(parts + LAGS[-1]):
@@ -715,7 +714,7 @@
             *[vmem((cycle[s], 3, blocks >> (s + 1), group_rows, 128)) for s in range(4)],
             vmem((16, model)),
             vmem((bits, 16, model)),
-            dma((16,)),
+            dma((18,)),
             dma((6,)),
             dma((6,)),
             pltpu.SemaphoreType.REGULAR,

time: 134 us -> 131 us (0.978)
  Pallas kernels: 133 us -> 130 us
    pallas_call x1, Pallas kernels: 129 us -> 126 us  [local_fused(): pl.pallas_call(lambda *refs: layer_kernel(wide, narrow, fields, patches,...]
where the time goes in v2:
time: 131 us
  Pallas kernels  130 us (99%)
    pallas_call x1, Pallas kernels, local_fused(): pl.pallas_call(lambda *refs: layer_kernel(wide, narrow, fields, patches,...  126 us
    pallas_call x1, Pallas kernels, local_fused(): pl.pallas_call(place_results, out_shape=[jax.ShapeDtypeStruct(array.shape...  3.83 us

profile of v2, /device:TPU:0, one launch (start us, length us, event | category | flops | bytes accessed | tf_op | source)
XLA Modules:
  0.0 131.0 jit_solution(10715208140807182173)
XLA Ops:
  0.7 126.3 %encoder_layer.1 = (bf16[512,768]{1,0:T(8,128)(2,1)}, f32[512,768]{1,0:T(8,128)}, f32[48,1152]{1,0:T(8,128)}, f32[48,384]{1,0:T(8,128)}, f32[48,1536]{1,0:T(8,12...) custom-call(bf16[512,768]{1,0:T(8,128)(2,1)} %bitcast.4, bf16[512,768]{1,0:T(8,128)(2,1)} %bitcast.5, ...), custom_call_target="tpu_custom_call" | custom-call | tf_op jit(solution)/shard_map/encoder_layer/pallas_call | solution.py:675
  127.0 3.8 %place_results.1 = (bf16[512,768]{1,0:T(8,128)(2,1)}, f32[512,768]{1,0:T(8,128)}, f32[48,1152]{1,0:T(8,128)}, f32[48,384]{1,0:T(8,128)}, f32[48,1536]{1,0:T(8,12...) custom-call(bf16[512,768]{1,0:T(8,128)(2,1)} %get-tuple-element.37.r, ...), custom_call_target="tpu_custom_call" | custom-call | tf_op jit(solution)/shard_map/place_results/pallas_call | solution.py:752

commit v3 on v2

--- a/solution.py
+++ b/solution.py
@@ -242,6 +242,29 @@
         for third in range(3):
             core_start(3 * unit + third)
 
+    def make_first_unit(rhs):
+        for part in range(3):
+            lhs = jnp.concatenate(
+                [
+                    left[pl.ds(row_block * block_rows + part * group_rows, group_rows), :]
+                    for row_block in range(wide)
+                ],
+                0,
+            )
+            product = dot(lhs, rhs())
+            kept, sent = kept_slot(part), sent_slot(part)
+            index = [kept + core * (sent - kept), sent + core * (kept - sent)]
+            for row_block in range(wide):
+                top = row_block * group_rows
+                for column_block in range(narrow):
+                    for group in range(3):
+                        where = place(part, group, row_block, column_block)
+                        side = column_block * width + group * 128
+                        keep[index[row_block % 2], group, where] = product[
+                            top : top + group_rows, side : side + 128
+                        ]
+            core_start(part)
+
     def row_of(vector):
         return vector[...].reshape(1, vector.shape[0])
 
@@ -368,7 +391,12 @@
     root = 0.7978845608028654
 
     def hidden_columns(part, column_block):
-        return pl.multiple_of(column_block * (hidden_width // narrow) + part * chunk, chunk)
+        first = column_block * (hidden_width // narrow) + part * chunk
+        return first if isinstance(first, int) else pl.multiple_of(first, chunk)
+
+    def block_start(column_block):
+        first = column_block * chunk
+        return first if isinstance(first, int) else pl.multiple_of(first, chunk)
 
     def each_block(step):
         def body(column_block, carry):
@@ -377,11 +405,11 @@
 
         lax.fori_loop(0, narrow, body, 0)
 
-    def feed(part):
+    def feed(part, step=each_block):
         def one(column_block):
             first = hidden_columns(part, column_block)
             columns = pl.ds(first, chunk)
-            here = pl.ds(pl.multiple_of(column_block * chunk, chunk), chunk)
+            here = pl.ds(block_start(column_block), chunk)
             hidden = dot(n2[...], w_a[:, columns]) + up_row[:, columns]
             pulled = dot_nt(cot[...], w_b[columns, :])
             square = hidden * hidden
@@ -397,7 +425,7 @@
             act_t[columns, :] = activated.T
             up_sums[:, columns] = column_sums(grad.astype(F32))
 
-        each_block(one)
+        step(one)
 
     def feed_sums(part):
         def one(column_block):
@@ -588,12 +616,14 @@
     up_load.wait()
     down_load.wait()
     cot_load.wait()
-    feed(0)
+    feed(0, lambda one: [one(column_block) for column_block in range(narrow)])
     pl.semaphore_wait(barrier, len(all_bits))
-    up_unit(0)
-    feed(1)
+    make_first_unit(lambda: hgrs[0])
+    feed(1, lambda one: one(0))
     core_end(0)
     core_end(1)
+    for column_block in range(1, narrow):
+        feed(1, lambda one: one(column_block))
     core_end(2)
     up_unit(1)
     vec_store = pltpu.make_async_copy(vec, vec_out, store_sem.at[2])

time: 131 us -> 131 us (level)
  no operation moved by 1% of the time
where the time goes in v3:
time: 131 us
  Pallas kernels  130 us (99%)
    pallas_call x1, Pallas kernels, local_fused(): pl.pallas_call(lambda *refs: layer_kernel(wide, narrow, fields, patches,...  126 us
    pallas_call x1, Pallas kernels, local_fused(): pl.pallas_call(place_results, out_shape=[jax.ShapeDtypeStruct(array.shape...  3.83 us

profile of v3, /device:TPU:0, one launch (start us, length us, event | category | flops | bytes accessed | tf_op | source)
XLA Modules:
  0.0 130.7 jit_solution(1337325172714368155)
XLA Ops:
  0.7 126.0 %encoder_layer.1 = (bf16[512,768]{1,0:T(8,128)(2,1)}, f32[512,768]{1,0:T(8,128)}, f32[48,1152]{1,0:T(8,128)}, f32[48,384]{1,0:T(8,128)}, f32[48,1536]{1,0:T(8,12...) custom-call(bf16[512,768]{1,0:T(8,128)(2,1)} %bitcast.4, bf16[512,768]{1,0:T(8,128)(2,1)} %bitcast.5, ...), custom_call_target="tpu_custom_call" | custom-call | tf_op jit(solution)/shard_map/encoder_layer/pallas_call | solution.py:705
  126.7 3.8 %place_results.1 = (bf16[512,768]{1,0:T(8,128)(2,1)}, f32[512,768]{1,0:T(8,128)}, f32[48,1152]{1,0:T(8,128)}, f32[48,384]{1,0:T(8,128)}, f32[48,1536]{1,0:T(8,12...) custom-call(bf16[512,768]{1,0:T(8,128)(2,1)} %get-tuple-element.37.r, ...), custom_call_target="tpu_custom_call" | custom-call | tf_op jit(solution)/shard_map/place_results/pallas_call | solution.py:782
